TPU v7x, 256 devices: a whole 4x4x8 slice. The times are simulated.
256 devices in a mesh: tmpl: 4 (over y_hi, core), row: 4 (over x), col: 16 (over z, y_lo).
Axes of the slice: x: 4, y: 4 (y_hi: 2, y_lo: 2; y = y_hi * 2 + y_lo), z: 8, core: 2. Of those that a mesh axis runs over, the one named last changes fastest.
Arguments:
- templ_pair: bfloat16 [4, 256, 256, 64], P('tmpl', 'row', 'col'), may hold values from -10 to 10
- main_pair: bfloat16 [256, 256, 128], P('row', 'col'), may hold values from -8 to 8
- coverage: int32 [4, 2], replicated, may hold values from 0 to 1
- pair_mask: int32 [2, 2], replicated, may hold values from 0 to 1
- tri_gain: float32 [64], replicated, may hold values from 0.1 to 1.9
- w_project: bfloat16 [64, 256], replicated, may hold values from -1 to 1
- w_bias: bfloat16 [64, 4], replicated, may hold values from -0.75 to 0.75
- w_tri_out: bfloat16 [64, 64], replicated, may hold values from -0.75 to 0.75
- merge_gain: float32 [64], replicated, may hold values from 0.1 to 1.9
- w_merge_q: bfloat16 [128, 64], replicated, may hold values from -1 to 1
- w_merge_kv: bfloat16 [64, 128], replicated, may hold values from -1 to 1
- w_merge_out: bfloat16 [64, 128], replicated, may hold values from -0.75 to 0.75
Outputs:
- templ_out: bfloat16 [4, 256, 256, 64], P('tmpl', 'row', 'col')
- embedding: bfloat16 [256, 256, 128], P('row', 'col')
All inputs are finite; a program needn't handle non-finite values.
Results may differ from a plain program's by a relative error of at most 0.015.
Values may be sent and summed in bfloat16 or wider, within the bound.
A program may use at most 64 MiB of HBM per device.

v0:
```python
import jax
import jax.numpy as jnp
from jax import lax
from jax.sharding import PartitionSpec as P

BLOCK = 128


MASK_SHIFT = 10000.0
EPSILON = 1e-05
NEG_START = -1e30


def layer_norm(values, scale_gain):
    values = values.astype(jnp.float32)
    center = values - jnp.mean(values, axis=-1, keepdims=True)
    spread = jnp.mean(center * center, axis=-1, keepdims=True)
    return center * lax.rsqrt(spread + EPSILON) * scale_gain


def row_group(rows_dev, cols_dev):
    chosen = 1
    for candidate in range(1, rows_dev + 1):
        if rows_dev % candidate == 0 and candidate * cols_dev <= 2048:
            chosen = candidate
    return chosen


def on_device(
    templ_pair,
    main_pair,
    coverage,
    pair_mask,
    tri_gain,
    w_project,
    w_bias,
    w_tri_out,
    merge_gain,
    w_merge_q,
    w_merge_kv,
    w_merge_out,
):
    pair_tile = templ_pair[0]
    rows_dev, cols_dev, channels = pair_tile.shape
    hidden = w_tri_out.shape[0]
    head_count = w_bias.shape[1]
    head_dim = hidden // head_count
    score_scale = head_dim ** (-0.5)
    row_start = lax.axis_index("row") * rows_dev
    col_start = lax.axis_index("col") * cols_dev
    templ_index = lax.axis_index("tmpl")
    cover_tok = jnp.repeat(coverage, BLOCK, axis=1)
    own_cover = lax.dynamic_index_in_dim(cover_tok, templ_index, 0, keepdims=False)
    mask_full = jnp.repeat(jnp.repeat(pair_mask, BLOCK, axis=0), BLOCK, axis=1)
    mask_rows = lax.dynamic_slice_in_dim(mask_full, row_start, rows_dev, 0)
    cover_rows = lax.dynamic_slice_in_dim(own_cover, row_start, rows_dev, 0)
    normed = layer_norm(pair_tile, tri_gain).astype(jnp.bfloat16)
    flat_norm = normed.reshape(-1, channels)
    w_query_gate = jnp.concatenate([w_project[:, :hidden], w_project[:, 3 * hidden :]], axis=1)
    query_gate = jnp.dot(flat_norm, w_query_gate, preferred_element_type=jnp.float32).reshape(
        rows_dev, cols_dev, 2 * hidden
    )
    queries = (
        (query_gate[..., :hidden] * score_scale)
        .astype(jnp.bfloat16)
        .reshape(rows_dev, cols_dev, head_count, head_dim)
    )
    gate_values = jax.nn.sigmoid(query_gate[..., hidden:])
    bias_tile = jnp.dot(flat_norm, w_bias, preferred_element_type=jnp.float32).astype(jnp.bfloat16)
    bias_tile = jnp.transpose(bias_tile.reshape(rows_dev, cols_dev, head_count), (2, 0, 1))
    bias_column = lax.all_gather(bias_tile, "row", axis=1, tiled=True)
    bias_slab = lax.all_to_all(bias_column, "col", split_axis=1, concat_axis=2, tiled=True)
    bias_rows = jnp.transpose(bias_slab, (1, 0, 2)).astype(jnp.float32)
    key_shift = MASK_SHIFT * (
        (cover_rows[:, None] * own_cover[None, :] * mask_rows).astype(jnp.float32) - 1.0
    )
    w_key_value = w_project[:, hidden : 3 * hidden]
    group = row_group(rows_dev, cols_dev)
    splits = rows_dev // group

    def grouped(array):
        return array.reshape((splits, group) + array.shape[1:])

    start_state = (
        jnp.full((rows_dev, cols_dev, head_count), NEG_START, jnp.float32),
        jnp.zeros((rows_dev, cols_dev, head_count), jnp.float32),
        jnp.zeros((rows_dev, cols_dev, head_count, head_dim), jnp.float32),
    )
    norm_piece = lax.all_gather(normed, "col", axis=1, tiled=True)
    piece_width = norm_piece.shape[1]

    def one_group(group_args):
        query_part, norm_part, shift_part, maxima, totals, weighted = group_args
        key_value = jnp.dot(
            norm_part.reshape(-1, channels), w_key_value, preferred_element_type=jnp.float32
        ).astype(jnp.bfloat16)
        key_value = key_value.reshape(group, piece_width, 2 * hidden)
        key_part = key_value[..., :hidden].reshape(group, piece_width, head_count, head_dim)
        value_part = key_value[..., hidden:].reshape(group, piece_width, head_count, head_dim)
        scores = jnp.einsum(
            "ijhd,ikhd->ijhk", query_part, key_part, preferred_element_type=jnp.float32
        )
        scores = scores + bias_rows[None] + shift_part[:, None, None, :]
        highest = jnp.maximum(maxima, jnp.max(scores, axis=-1))
        rescale = jnp.exp(maxima - highest)
        weights = jnp.exp(scores - highest[..., None])
        totals = totals * rescale + jnp.sum(weights, axis=-1)
        summed = jnp.einsum(
            "ijhk,ikhd->ijhd",
            weights.astype(jnp.bfloat16),
            value_part,
            preferred_element_type=jnp.float32,
        )
        weighted = weighted * rescale[..., None] + summed
        return (highest, totals, weighted)

    outcome = lax.map(
        one_group,
        (
            grouped(queries),
            grouped(norm_piece),
            grouped(key_shift),
            grouped(start_state[0]),
            grouped(start_state[1]),
            grouped(start_state[2]),
        ),
    )
    result = tuple((member.reshape((rows_dev,) + member.shape[2:]) for member in outcome))
    attended = result[2] / result[1][..., None]
    gated = (attended.reshape(rows_dev, cols_dev, hidden) * gate_values).astype(jnp.bfloat16)
    projected = jnp.dot(
        gated.reshape(-1, hidden), w_tri_out, preferred_element_type=jnp.float32
    ).reshape(rows_dev, cols_dev, channels)
    new_pair = (pair_tile.astype(jnp.float32) + projected).astype(jnp.bfloat16)
    merge_norm = layer_norm(new_pair, merge_gain).astype(jnp.bfloat16)
    merge_kv = jnp.dot(
        merge_norm.reshape(-1, channels), w_merge_kv, preferred_element_type=jnp.float32
    ).astype(jnp.bfloat16)
    merge_kv = merge_kv.reshape(rows_dev, cols_dev, 2 * hidden)
    pair_ch = main_pair.shape[-1]
    main_query = (
        jnp.dot(main_pair.reshape(-1, pair_ch), w_merge_q, preferred_element_type=jnp.float32)
        * score_scale
    )
    main_query = main_query.reshape(rows_dev, cols_dev, head_count, head_dim)
    mask_tile = lax.dynamic_slice_in_dim(mask_rows, col_start, cols_dev, 1)
    everyone = lax.all_gather(merge_kv[None], "tmpl", axis=0, tiled=True)
    keys_all = (
        everyone[..., :hidden]
        .astype(jnp.float32)
        .reshape(-1, rows_dev, cols_dev, head_count, head_dim)
    )
    values_all = (
        everyone[..., hidden:]
        .astype(jnp.float32)
        .reshape(-1, rows_dev, cols_dev, head_count, head_dim)
    )
    cover_rows_all = lax.dynamic_slice_in_dim(cover_tok, row_start, rows_dev, 1)
    cover_cols_all = lax.dynamic_slice_in_dim(cover_tok, col_start, cols_dev, 1)
    valid_mask = cover_rows_all[:, :, None] * cover_cols_all[:, None, :] * mask_tile[None]
    shift_bias = MASK_SHIFT * (valid_mask.astype(jnp.float32) - 1.0)
    scores = jnp.sum(main_query[None] * keys_all, axis=-1) + shift_bias[..., None]
    highest = jnp.max(scores, axis=0, keepdims=True)
    weights = jnp.exp(scores - highest)
    totals = jnp.sum(weights, axis=0)
    merged = jnp.sum(weights[..., None] * values_all, axis=0) / totals[..., None]
    merged = merged.reshape(-1, hidden).astype(jnp.bfloat16)
    embedding = jnp.dot(merged, w_merge_out, preferred_element_type=jnp.float32).astype(
        jnp.bfloat16
    )
    return (new_pair[None], embedding.reshape(rows_dev, cols_dev, pair_ch))


def solution(mesh):
    in_specs = (
        P("tmpl", "row", "col", None),
        P("row", "col", None),
        P(),
        P(),
        P(),
        P(),
        P(),
        P(),
        P(),
        P(),
        P(),
        P(),
    )
    out_specs = (P("tmpl", "row", "col", None), P("row", "col", None))
    return jax.shard_map(
        on_device, mesh=mesh, in_specs=in_specs, out_specs=out_specs, check_vma=False
    )
```

profile of v0, /device:TPU:1, one launch (start us, length us, event | category | flops | bytes accessed | tf_op | source)
XLA Modules:
  0.0 191.7 jit_solution(9202930397747794624)
XLA Ops:
  7.3 1.3 copy.73
  9.5 0.8 copy.74
  11.0 1.0 fusion.28
  12.9 11.0 %all_gather.10 = bf16[4,256,16]{2,1,0:T(8,128)(2,1)S(1)} all-gather(bf16[4,64,16]{2,1,0:T(8,128)(2,1)S(1)} %bitcast.131), channel_id=1, replica_groups=mesh['tmpl'=4,'row'=4,'col'=16] {'row'}, dimensions={1}, use_global_device_ids=true | all-gather | bytes 40960 | tf_op jit(solution)/shard_map/all_gather | solution.py:71
  24.1 0.9 reshape.195
  25.0 9.3 %all-to-all-start = ((bf16[16,2,512]{2,1,0:T(2,128)(2,1)}), bf16[16,2,512]{2,1,0:T(2,128)(2,1)S(1)}, u32[]{:S(2)}, u32[]{:S(2)}) async-start(bf16[16,2,512]{2,1,0:T(2,128)(2,1)} %reshape.195), calls=%async_computation | async-start | bytes 65536 | tf_op jit(solution)/shard_map/all_to_all | solution.py:72
  36.3 2.6 %copy.79 = bf16[64,16,4,16]{3,1,2,0:T(8,128)(2,1)} copy(bf16[64,16,4,16]{0,3,2,1:T(8,128)(2,1)S(1)} %bitcast.119) | data formatting | bytes 262144 | tf_op jit(solution)/shard_map/while/body/jit(dynamic_index_in_dim)/squeeze | solution.py:117
  38.9 3.1 %all-to-all-done = bf16[16,2,512]{2,1,0:T(2,128)(2,1)S(1)} async-done(((bf16[16,2,512]{2,1,0:T(2,128)(2,1)}), bf16[16,2,512]{2,1,0:T(2,128)(2,1)S(1)}, u32[]{:S(2)}, u32[]{:S(2)}) %all-to-all-start) | async-done | bytes 32800 | tf_op jit(solution)/shard_map/all_to_all | solution.py:72
  42.9 69.8 %all-gather.3.cloned.1.call-done = bf16[64,256,64]{2,0,1:T(8,128)(2,1)} async-done(((bf16[64,16,64]{2,0,1:T(8,128)(2,1)}), bf16[64,256,64]{2,0,1:T(8,128)(2,1)}) %all-gather.3.cloned.1.call-update) | async-done | bytes 2097168 | tf_op jit(solution)/shard_map/all_gather | solution.py:89
  112.7 7.0 %copy.75 = bf16[64,256,64]{1,0,2:T(8,128)(2,1)S(1)} copy(bf16[64,256,64]{2,0,1:T(8,128)(2,1)} %all-gather.3.cloned.1.call-done) | data formatting | bytes 4194304 | tf_op jit(solution)/shard_map/all_gather | solution.py:89
  119.7 1.3 copy.106
  120.9 1.3 convolution_convert_fusion
  122.3 4.2 %fusion.39 = (bf16[64,256,64]{2,1,0:T(8,128)(2,1)}, bf16[64,256,64]{2,1,0:T(8,128)(2,1)}) fusion(bf16[64,256,128]{2,1,0:T(8,128)(2,1)S(1)} %bitcast.112), kind=kLoop, calls=%fused_computation.76 | loop fusion | bytes 8388608 | tf_op jit(solution)/shard_map/while/body/eval_jaxpr/slice | solution.py:99
  126.5 3.5 %copy.76 = bf16[64,256,64]{1,2,0:T(8,128)(2,1)S(1)} copy(bf16[64,256,64]{2,1,0:T(8,128)(2,1)} %get-tuple-element.37) | data formatting | bytes 4194304 | tf_op jit(solution)/shard_map/while/body/eval_jaxpr/slice | solution.py:98
  130.0 2.0 %fusion.3 = (f32[64,16,4]{1,2,0:T(4,128)S(1)}, f32[64,4,256,16]{2,3,1,0:T(8,128)S(1)}) fusion(f32[64,256]{1,0:T(8,128)S(1)} %add_multiply_fusion, f32[16,4,256]{2,0,1:T(8,128)S(1)} %bitcast.125, bf16[64,16,4,16]{3,1,2,0:T(8,128)(2,1)} %copy.79, bf16[64,256,4,16]{1,3,2,0:T(8,128)(2,1)S(1)} %bitcast.115), kind=kOutput, calls=%fused_computation.6 | convolution fusion | flops 36696064 | bytes 6569984 | tf_op jit(solution)/shard_map/while/body/eval_jaxpr/ijhd,ikhd->ijhk/dot_general | solution.py:100
  132.1 1.9 copy-done.1
  134.0 2.0 %fusion.1 = f32[64,16,4]{1,2,0:T(4,128)S(1)} fusion(f32[64,4,256,16]{2,3,1,0:T(8,128)S(1)} %get-tuple-element.45, f32[64,16,4]{1,2,0:T(4,128)S(1)} %broadcast_maximum_fusion, f32[64,256]{1,0:T(8,128)S(1)} %add_multiply_fusion, f32[16,4,256]{2,0,1:T(8,128)S(1)} %bitcast.126), kind=kLoop, calls=%fused_computation.4 | loop fusion | flops 4190208 | bytes 4358144 | tf_op jit(solution)/shard_map/while/body/eval_jaxpr/reduce_sum | solution.py:107
  136.8 3.5 %copy.86 = bf16[64,256,64]{1,2,0:T(8,128)(2,1)S(1)} copy(bf16[64,256,64]{2,1,0:T(8,128)(2,1)} %get-tuple-element.36) | data formatting | bytes 4194304 | tf_op jit(solution)/shard_map/while/body/eval_jaxpr/slice | solution.py:99
  140.3 4.6 %fusion.8 = f32[64,16,4,16]{1,3,2,0:T(8,128)} fusion(f32[64,16,4]{1,2,0:T(4,128)} %get-tuple-element.41, f32[64,16,4]{1,2,0:T(4,128)S(1)} %get-tuple-element.40, bf16[64,256,4,16]{1,3,2,0:T(8,128)(2,1)S(1)} %bitcast.117, f32[64,4,256,16]{2,3,1,0:T(8,128)} %copy-done.1, f32[64,16,4]{1,2,0:T(4,128)S(1)} %broadcast_maximum_fusion, ...), kind=kOutput, calls=%fused_computation.13 | convolution fusion | flops 37879808 | bytes 6733824 | tf_op jit(solution)/shard_map/while/body/eval_jaxpr/ijhk,ikhd->ijhd/dot_general | solution.py:108
  144.9 2.2 %copy.88 = f32[64,16,64]{2,1,0:T(8,128)S(1)} copy(f32[64,16,64]{1,2,0:T(8,128)} %bitcast.118) | data formatting | bytes 524288 | tf_op jit(solution)/shard_map/div | solution.py:129
  147.4 1.1 convert_reduce_fusion
  149.1 0.9 convolution_convert_fusion.2
  150.9 1.5 copy.91
  152.4 1.0 dynamic_slice.41
  153.7 0.9 copy.99
  154.6 20.4 %all-gather.5.cloned.1.call-done = bf16[4,64,16,128]{3,2,1,0:T(8,128)(2,1)} async-done(((bf16[1,64,16,128]{3,2,1,0:T(8,128)(2,1)}), bf16[4,64,16,128]{3,2,1,0:T(8,128)(2,1)}) %all-gather.5.cloned.1.call-update) | async-done | bytes 1048592 | tf_op jit(solution)/shard_map/all_gather | solution.py:147
  175.1 2.0 %fusion.40 = (bf16[4,64,16,64]{3,2,1,0:T(8,128)(2,1)S(1)}, bf16[4,64,16,64]{3,2,1,0:T(8,128)(2,1)S(1)}) fusion(bf16[4,64,16,128]{3,2,1,0:T(8,128)(2,1)} %all-gather.5.cloned.1.call-done), kind=kLoop, calls=%fused_computation.77 | loop fusion | bytes 2097152 | tf_op jit(solution)/shard_map/slice | solution.py:154
  177.1 1.3 copy.104
  178.4 1.6 fusion.6
  180.1 1.0 copy.105
  182.1 1.6 div.50
  183.9 0.9 convolution_convert_fusion.1
  (76 shorter events, 9.5 us)
Async XLA Ops:
  7.2 142.8 %copy-start = (bf16[64,16,128]{2,1,0:T(8,128)(2,1)S(1)}, bf16[64,16,128]{2,1,0:T(8,128)(2,1)}, u32[]{:S(2)}) copy-start(bf16[64,16,128]{2,1,0:T(8,128)(2,1)} %param.13) | copy-start | bytes 786436
  7.2 27.5 %copy-start.8 = (s32[4,2]{0,1:T(2,128)S(1)}, s32[4,2]{0,1:T(2,128)}, u32[]{:S(2)}) copy-start(s32[4,2]{0,1:T(2,128)} %param.14) | copy-start | bytes 100
  7.2 27.6 %copy-start.7 = (s32[2,2]{1,0:T(2,128)S(1)}, s32[2,2]{1,0:T(2,128)}, u32[]{:S(2)}) copy-start(s32[2,2]{1,0:T(2,128)} %param.15) | copy-start | bytes 52
  7.2 28.1 %copy-start.3 = (bf16[64,256]{1,0:T(8,128)(2,1)S(1)}, bf16[64,256]{1,0:T(8,128)(2,1)}, u32[]{:S(2)}) copy-start(bf16[64,256]{1,0:T(8,128)(2,1)} %param.17) | copy-start | bytes 98308
  7.2 105.4 %all-gather.3.cloned.1.call-start = ((), (), s32[]{:S(2)}) async-start(), calls=%async_computation.1 | async-start | bytes 4456448 | tf_op jit(solution)/shard_map/all_gather | solution.py:89
  25.0 17.1 %all-to-all-start = ((bf16[16,2,512]{2,1,0:T(2,128)(2,1)}), bf16[16,2,512]{2,1,0:T(2,128)(2,1)S(1)}, u32[]{:S(2)}, u32[]{:S(2)}) async-start(bf16[16,2,512]{2,1,0:T(2,128)(2,1)} %reshape.195), calls=%async_computation | async-start | bytes 65536 | tf_op jit(solution)/shard_map/all_to_all | solution.py:72
  34.3 140.7 %all-gather.5.cloned.1.call-start = ((), (), s32[]{:S(2)}) async-start(), calls=%async_computation.2 | async-start | bytes 1310720 | tf_op jit(solution)/shard_map/all_gather | solution.py:147
  35.2 0.7 copy-start.2
  132.1 2.0 %copy-start.1 = (f32[64,4,256,16]{2,3,1,0:T(8,128)}, f32[64,4,256,16]{2,3,1,0:T(8,128)S(1)}, u32[]{:S(2)}) copy-start(f32[64,4,256,16]{2,3,1,0:T(8,128)S(1)} %get-tuple-element.45) | copy-start | bytes 12582916
  144.9 3.7 %copy-start.9 = (f32[64]{0:T(128)S(1)}, f32[64]{0:T(128)}, u32[]{:S(2)}) copy-start(f32[64]{0:T(128)} %param.20) | copy-start | bytes 772
  144.9 4.1 %copy-start.4 = (bf16[64,128]{1,0:T(8,128)(2,1)S(1)}, bf16[64,128]{1,0:T(8,128)(2,1)}, u32[]{:S(2)}) copy-start(bf16[64,128]{1,0:T(8,128)(2,1)} %param.22) | copy-start | bytes 49156
  144.9 5.1 %copy-start.5 = (bf16[128,64]{0,1:T(8,128)(2,1)S(1)}, bf16[128,64]{0,1:T(8,128)(2,1)}, u32[]{:S(2)}) copy-start(bf16[128,64]{0,1:T(8,128)(2,1)} %param.21) | copy-start | bytes 49156
  181.4 2.5 %copy-start.6 = (bf16[64,128]{1,0:T(8,128)(2,1)S(1)}, bf16[64,128]{1,0:T(8,128)(2,1)}, u32[]{:S(2)}) copy-start(bf16[64,128]{1,0:T(8,128)(2,1)} %param.23) | copy-start | bytes 49156
Sparse Core Ops, SparseCore 0:
  10.5 102.1 all-gather.2
  150.1 24.9 all-gather.4
where the time goes:
time: 192 us
  waiting for transfers between devices  93.3 us (49%)
  local copies, waits for them, and re-layouts  43.7 us (23%)
  between operations  14.5 us (8%)
  matrix products  12.3 us (6%)
  blocking collectives  11 us (6%)
  starting transfers between devices  9.38 us (5%)
  other arithmetic  7.53 us (4%)
    all_gather x1, waiting for transfers between devices, on_device(): norm_piece = lax.all_gather(normed, 'col', axis=1, tiled=True)  69.8 us
    all_gather x1, waiting for transfers between devices, on_device(): everyone = lax.all_gather(merge_kv[None], 'tmpl', axis=0, tiled=True)  20.4 us
    all_gather x1, blocking collectives, on_device(): bias_column = lax.all_gather(bias_tile, 'row', axis=1, tiled=True)  11 us
    all_to_all x1, starting transfers between devices, on_device(): lax.all_to_all(bias_column, 'col', split_axis=1, concat_axis=2, tiled=True)  9.3 us
    unnamed x31, local copies, waits for them, and re-layouts  9.2 us
    slice x2, local copies, waits for them, and re-layouts, one_group(): key_value[..., hidden:].reshape(group, piece_width, head_count, head_dim)  7.73 us
    all_gather x1, local copies, waits for them, and re-layouts, on_device(): norm_piece = lax.all_gather(normed, 'col', axis=1, tiled=True)  6.99 us
    dot_general x1, matrix products, one_group(): jnp.einsum('ijhk,ikhd->ijhd', weights.astype(jnp.bfloat16), value_part, p...  4.64 us
  transfers between devices with their start and end apart: 3, of which 3 were waited for; matrix products, arithmetic and copies ran while one was open for 7% of the time, Pallas kernels for 0%

commit v1 on v0

v1 whole, which is shorter than its diff:
```python
import jax
import jax.numpy as jnp
from jax import lax
from jax.experimental import pallas as pl
from jax.experimental.pallas import tpu as pltpu
from jax.sharding import PartitionSpec as P

MASK_SHIFT = 10000.0
EPSILON = 1e-05
MESH = pl.DeviceIdType.MESH
F32 = jnp.float32
BF16 = jnp.bfloat16


def iota(shape, axis):
    return lax.broadcasted_iota(jnp.int32, shape, axis)


def dot_nn(a, b):
    return lax.dot_general(a, b, (((1,), (0,)), ((), ())), preferred_element_type=F32)


def dot_nt(a, b):
    return lax.dot_general(a, b, (((1,), (1,)), ((), ())), preferred_element_type=F32)


def dot_tn(a, b):
    return lax.dot_general(a, b, (((0,), (0,)), ((), ())), preferred_element_type=F32)


def split_dot(values, weights):
    high = values.astype(BF16)
    low = (values - high.astype(F32)).astype(BF16)
    return dot_nn(high, weights) + dot_nn(low, weights)


def pair_norm(values, averager, gain):
    center = values.astype(F32) - dot_nn(values, averager)
    spread = split_dot(center * center, averager)
    return (center * lax.rsqrt(spread + EPSILON) * gain).astype(BF16)


def ones_where(condition):
    return jnp.where(condition, 1.0, 0.0).astype(BF16)


def diagonal(doubled):
    both = jnp.concatenate([doubled, doubled], axis=0)
    keep = (iota((128, 128), 0) < 64) == (iota((128, 128), 1) < 64)
    return jnp.where(keep, both, 0.0).astype(BF16)


def pick_columns(width, first):
    return ones_where(iota((width, 128), 0) == first + iota((width, 128), 1) % 64)


def pair_kernel(
    templ_ref,
    main_ref,
    coverage_ref,
    mask_ref,
    tri_gain_ref,
    w_project_ref,
    w_bias_ref,
    w_tri_ref,
    merge_gain_ref,
    w_query_ref,
    w_kv_ref,
    new_out,
    merged_out,
    tile,
    packed,
    rows_in,
    bias_tile,
    bias_in,
    bias_full,
    main_in,
    normed,
    fresh,
    peers_in,
    merged,
    sizes,
    load_sem,
    rows_send,
    rows_recv,
    bias_send,
    bias_recv,
    main_send,
    main_recv,
    peer_send,
    peer_recv,
    new_send,
    new_recv,
    merged_send,
    merged_recv,
    second_sem,
):
    templ = lax.axis_index("tmpl")
    row = lax.axis_index("row")
    col = lax.axis_index("col")
    plane, half = col // 2, col % 2
    col_half = col // 8

    load = pltpu.make_async_copy(templ_ref, tile, load_sem)
    load.start()

    barrier = pltpu.get_barrier_semaphore()
    for step in range(1, 16):
        pl.semaphore_signal(barrier, inc=1, device_id=(templ, row, (col + step) % 16), device_id_type=MESH)
    for step in range(1, 4):
        pl.semaphore_signal(barrier, inc=1, device_id=(templ, (row + step) % 4, col), device_id_type=MESH)
        pl.semaphore_signal(barrier, inc=1, device_id=((templ + step) % 4, row, col), device_id_type=MESH)

    load.wait()
    eye = iota((64, 128), 0)
    lane = iota((64, 128), 1)
    low_rows = tile[pl.ds(0, 32)].reshape(512, 64)
    high_rows = tile[pl.ds(32, 32)].reshape(512, 64)
    together = dot_nn(low_rows, ones_where(eye == lane)) + dot_nn(high_rows, ones_where(eye + 64 == lane))
    packed[...] = together.astype(BF16).reshape(32, 16, 128)

    pl.semaphore_wait(barrier, 21)
    for step in range(1, 4):
        pl.semaphore_signal(second_sem, inc=1, device_id=(templ, (row + step) % 4, col), device_id_type=MESH)
        pl.semaphore_signal(second_sem, inc=1, device_id=((templ + step) % 4, row, col), device_id_type=MESH)

    own_rows = pltpu.make_async_copy(
        packed.at[pl.ds(4 * plane, 4)], rows_in.at[:, pl.ds(pl.multiple_of(16 * col, 16), 16), :], rows_recv
    )
    own_rows.start()

    def send_rows(step, carry):
        to = (col + step) % 16
        pltpu.make_async_remote_copy(
            src_ref=packed.at[pl.ds(4 * (to // 2), 4)],
            dst_ref=rows_in.at[:, pl.ds(pl.multiple_of(16 * col, 16), 16), :],
            send_sem=rows_send,
            recv_sem=rows_recv,
            device_id=(templ, row, to),
            device_id_type=MESH,
        ).start()
        return carry

    lax.fori_loop(1, 16, send_rows, 0)

    averager = jnp.where(
        (iota((128, 128), 0) < 64) == (iota((128, 128), 1) < 64), 1.0 / 64, 0.0
    ).astype(BF16)
    tri_gain = jnp.concatenate([tri_gain_ref[...], tri_gain_ref[...]], axis=1)
    own_normed = pair_norm(packed[...].reshape(512, 128), averager, tri_gain)

    w_bias = dot_nn(w_bias_ref[...], pick_columns(64, 0))
    which = iota((256, 128), 0)
    spread_bias = jnp.zeros((256, 128), F32)
    for head in range(4):
        spread_bias = jnp.where(which // 64 == head, w_bias[head : head + 1, :], spread_bias)
    spread_bias = jnp.where((which // 32) % 2 == iota((256, 128), 1) // 64, spread_bias, 0.0).astype(BF16)
    every_bias = dot_nt(own_normed, spread_bias).reshape(32, 16, 256)
    place = iota((16, 256), 1) % 32
    chosen = jnp.zeros((16, 256), F32)
    for index in range(32):
        chosen = jnp.where(place == index, every_bias[index], chosen)
    chosen = chosen.astype(BF16)
    bias_tile[0] = chosen[:, :128]
    bias_tile[1] = chosen[:, 128:]

    pl.semaphore_wait(second_sem, 6)
    bias_half = row // 2

    def bias_place():
        return bias_in.at[row % 2, :, pl.ds(pl.multiple_of(16 * col, 16), 16), :]

    def send_bias(step, carry):
        to_row, to_plane = (row + step) % 4, (plane + step // 4) % 8
        to_col = 2 * to_plane + bias_half
        here = (to_row == row) & (to_col == col)

        @pl.when(here)
        def _():
            pltpu.make_async_copy(bias_tile, bias_place(), bias_recv).start()

        @pl.when(jnp.logical_not(here))
        def _():
            pltpu.make_async_remote_copy(
                src_ref=bias_tile,
                dst_ref=bias_place(),
                send_sem=bias_send,
                recv_sem=bias_recv,
                device_id=(templ, to_row, to_col),
                device_id_type=MESH,
            ).start()

        return carry

    lax.fori_loop(0, 32, send_bias, 0)

    def main_place():
        return main_in.at[:, pl.ds(pl.multiple_of(16 * (col % 8), 16), 16), :]

    def send_main(step, carry):
        to_plane = (plane + step) % 8
        to_col = 2 * to_plane + col_half
        here = to_col == col
        source = main_ref.at[:, 4 * to_plane + templ]

        @pl.when(here)
        def _():
            pltpu.make_async_copy(source, main_place(), main_recv).start()

        @pl.when(jnp.logical_not(here))
        def _():
            pltpu.make_async_remote_copy(
                src_ref=source,
                dst_ref=main_place(),
                send_sem=main_send,
                recv_sem=main_recv,
                device_id=(templ, row, to_col),
                device_id_type=MESH,
            ).start()

        return carry

    lax.fori_loop(0, 8, send_main, 0)

    w_project = w_project_ref[...]
    double = pick_columns(64, 0)

    def turned(first):
        columns = ones_where(iota((128, 256), 1) == first + iota((128, 256), 0) % 64)
        wide = dot_nn(dot_nt(columns, w_project).astype(BF16), double)
        keep = (iota((128, 128), 0) < 64) == (iota((128, 128), 1) < 64)
        return jnp.where(keep, wide, 0.0).astype(BF16)

    turned_query, turned_value, turned_gate = turned(0), turned(128), turned(192)
    w_key = diagonal(dot_nn(w_project, pick_columns(256, 64)))
    w_tri = diagonal(dot_nn(w_tri_ref[...], double))
    ones_rows = jnp.ones((16, 256), BF16)
    head_of = iota((128, 128), 0) // 16

    row_block = row // 2
    cover_row = coverage_ref[row_block, templ]
    shift_low = MASK_SHIFT * ((cover_row * coverage_ref[0, templ] * mask_ref[row_block, 0]).astype(F32) - 1.0)
    shift_high = MASK_SHIFT * ((cover_row * coverage_ref[1, templ] * mask_ref[row_block, 1]).astype(F32) - 1.0)
    gap = shift_high - shift_low

    pltpu.make_async_copy(bias_in, bias_in, bias_recv).wait()
    first_half = iota((256, 128), 1) < 64
    for pair in range(2):
        one = bias_in[0, pair].astype(F32)
        two = bias_in[1, pair].astype(F32)
        bias_full[2 * pair] = jnp.where(first_half, one, pltpu.roll(two, 64, 1))
        bias_full[2 * pair + 1] = jnp.where(first_half, pltpu.roll(one, 64, 1), two)

    pltpu.make_async_copy(rows_in, rows_in, rows_recv).wait()
    mine = pl.ds(pl.multiple_of(128 * half, 128), 128)

    def attend(step, carry):
        pair = (templ + 1 + step) % 4
        normed_all = pair_norm(rows_in[pair], averager, tri_gain)
        normed[...] = normed_all
        keys = dot_nn(normed_all, w_key).astype(BF16)
        values = dot_nt(turned_value, normed_all).astype(BF16)
        normed_mine = normed[mine, :]
        queries = (dot_nt(turned_query, normed_mine) * 0.25).astype(BF16)
        gates = jax.nn.sigmoid(dot_nt(turned_gate, normed_mine))
        parts = []
        for index in range(8):
            alone = jnp.where(head_of == index, queries, jnp.zeros_like(queries))
            scores = dot_nn(keys, alone) + bias_full[index % 4]
            low, high = scores[:128], scores[128:]
            top_low = jnp.max(low, axis=0, keepdims=True)
            top_high = jnp.max(high, axis=0, keepdims=True)
            weights = jnp.concatenate(
                [
                    jnp.exp(low - jnp.maximum(top_low, top_high + gap)),
                    jnp.exp(high - jnp.maximum(top_low - gap, top_high)),
                ],
                axis=0,
            ).astype(BF16)
            mixed = dot_nn(
                jnp.concatenate([values[16 * index : 16 * index + 16], ones_rows], axis=0), weights
            )
            parts.append(mixed[:16] / mixed[16:])
        gated = (jnp.concatenate(parts, axis=0) * gates).astype(BF16)
        projected = dot_tn(gated, w_tri)
        result = (rows_in[pair, mine, :].astype(F32) + projected).astype(BF16)
        fresh[pair] = result

        @pl.when(pair == templ)
        def _():
            peers_in[templ] = result

        @pl.when(pair != templ)
        def _():
            pltpu.make_async_remote_copy(
                src_ref=fresh.at[pair],
                dst_ref=peers_in.at[templ],
                send_sem=peer_send.at[step],
                recv_sem=peer_recv.at[templ],
                device_id=(pair, row, col),
                device_id_type=MESH,
            ).start()

        def send_new(index, inner):
            to_col = 8 * half + (col + index) % 8
            source = fresh.at[pair, pl.ds(pl.multiple_of(16 * ((col + index) % 8), 16), 16), :]

            @pl.when(to_col == col)
            def _():
                pltpu.make_async_copy(source, new_out.at[4 * plane + pair], new_recv).start()

            @pl.when(to_col != col)
            def _():
                pltpu.make_async_remote_copy(
                    src_ref=source,
                    dst_ref=new_out.at[4 * plane + pair],
                    send_sem=new_send,
                    recv_sem=new_recv,
                    device_id=(templ, row, to_col),
                    device_id_type=MESH,
                ).start()

            return inner

        lax.fori_loop(0, 8, send_new, 0)
        return carry

    lax.fori_loop(0, 4, attend, 0)

    pltpu.make_async_copy(main_in, main_in, main_recv).wait()
    w_query = w_query_ref[...]
    nothing = jnp.zeros_like(w_query)
    main_query = 0.25 * (
        dot_nt(main_in[0], jnp.concatenate([w_query, nothing], axis=0))
        + dot_nt(main_in[1], jnp.concatenate([nothing, w_query], axis=0))
    )
    w_kv = w_kv_ref[...]
    w_merge_key = diagonal(dot_nn(w_kv, pick_columns(128, 0)))
    w_merge_value = diagonal(dot_nn(w_kv, pick_columns(128, 64)))
    merge_gain = jnp.concatenate([merge_gain_ref[...], merge_gain_ref[...]], axis=1)
    summer = ones_where(iota((128, 128), 0) // 16 == iota((128, 128), 1) // 16)

    def wait_peer(step, carry):
        source = (templ + step) % 4
        pltpu.make_async_copy(peers_in.at[source], peers_in.at[source], peer_recv.at[source]).wait()
        return carry

    lax.fori_loop(1, 4, wait_peer, 0)
    scores = []
    shown = []
    for other in range(4):
        other_normed = pair_norm(peers_in[other], averager, merge_gain)
        merge_keys = dot_nn(other_normed, w_merge_key).astype(BF16).astype(F32)
        shown.append(dot_nn(other_normed, w_merge_value).astype(BF16).astype(F32))
        valid = coverage_ref[row_block, other] * coverage_ref[half, other] * mask_ref[row_block, half]
        scores.append(split_dot(main_query * merge_keys, summer) + MASK_SHIFT * (valid.astype(F32) - 1.0))
    highest = jnp.maximum(jnp.maximum(scores[0], scores[1]), jnp.maximum(scores[2], scores[3]))
    weights = [jnp.exp(score - highest) for score in scores]
    total = (weights[0] + weights[1]) + (weights[2] + weights[3])
    blend = (weights[0] * shown[0] + weights[1] * shown[1]) + (weights[2] * shown[2] + weights[3] * shown[3])
    merged[...] = (blend / total).astype(BF16)

    def send_merged(step, carry):
        to_templ = (templ + step) % 4
        to_col = 8 * half + (col + step // 4) % 8
        here = (to_templ == templ) & (to_col == col)
        source = merged.at[pl.ds(pl.multiple_of(16 * ((col + step // 4) % 8), 16), 16), :]

        @pl.when(here)
        def _():
            pltpu.make_async_copy(source, merged_out.at[4 * plane + templ], merged_recv).start()

        @pl.when(jnp.logical_not(here))
        def _():
            pltpu.make_async_remote_copy(
                src_ref=source,
                dst_ref=merged_out.at[4 * plane + templ],
                send_sem=merged_send,
                recv_sem=merged_recv,
                device_id=(to_templ, row, to_col),
                device_id_type=MESH,
            ).start()

        return carry

    lax.fori_loop(0, 32, send_merged, 0)

    def drain(ref, sem):
        pltpu.make_async_copy(ref, ref, sem).wait()

    for step in range(3):
        drain(fresh.at[0], peer_send.at[step])
    drain(sizes.at[pl.ds(0, 30)], rows_send)
    to_self = col_half == half

    @pl.when(bias_half == half)
    def _():
        drain(sizes.at[pl.ds(0, 31)], bias_send)

    @pl.when(bias_half != half)
    def _():
        drain(sizes.at[pl.ds(0, 32)], bias_send)

    @pl.when(to_self)
    def _():
        drain(sizes.at[pl.ds(0, 7)], main_send)
        drain(sizes.at[pl.ds(0, 14)], new_send)
        drain(packed.at[pl.ds(0, 31)], merged_send)

    @pl.when(jnp.logical_not(to_self))
    def _():
        drain(sizes.at[pl.ds(0, 8)], main_send)
        drain(sizes.at[pl.ds(0, 16)], new_send)
        drain(packed.at[pl.ds(0, 32)], merged_send)

    drain(new_out, new_recv)
    drain(merged_out, merged_recv)


def out_kernel(new_ref, merged_ref, w_out_ref, templ_ref, embedding_ref):
    new = new_ref[...]
    templ_ref[0, pl.ds(0, 32)] = new[:, :, :64]
    templ_ref[0, pl.ds(32, 32)] = new[:, :, 64:]
    merged = merged_ref[...].reshape(512, 128)
    w_out = w_out_ref[...]
    nothing = jnp.zeros_like(w_out)
    first = dot_nn(merged, jnp.concatenate([w_out, nothing], axis=0))
    second = dot_nn(merged, jnp.concatenate([nothing, w_out], axis=0))
    embedding_ref[pl.ds(0, 32)] = first.astype(BF16).reshape(32, 16, 128)
    embedding_ref[pl.ds(32, 32)] = second.astype(BF16).reshape(32, 16, 128)


def on_device(
    templ_pair,
    main_pair,
    coverage,
    pair_mask,
    tri_gain,
    w_project,
    w_bias,
    w_tri_out,
    merge_gain,
    w_merge_q,
    w_merge_kv,
    w_merge_out,
):
    vmem = pl.BlockSpec(memory_space=pltpu.VMEM)
    smem = pl.BlockSpec(memory_space=pltpu.SMEM)
    anywhere = pl.BlockSpec(memory_space=pl.ANY)
    piece = jax.ShapeDtypeStruct((32, 16, 128), BF16)
    dma = pltpu.SemaphoreType.DMA
    new, merged = pl.pallas_call(
        pair_kernel,
        out_shape=(piece, piece),
        in_specs=[anywhere, anywhere, smem, smem] + [vmem] * 7,
        out_specs=(anywhere, anywhere),
        scratch_shapes=[
            pltpu.VMEM((64, 16, 64), BF16),
            pltpu.VMEM((32, 16, 128), BF16),
            pltpu.VMEM((4, 256, 128), BF16),
            pltpu.VMEM((2, 16, 128), BF16),
            pltpu.VMEM((2, 2, 256, 128), BF16),
            pltpu.VMEM((4, 256, 128), F32),
            pltpu.VMEM((2, 128, 128), BF16),
            pltpu.VMEM((256, 128), BF16),
            pltpu.VMEM((4, 128, 128), BF16),
            pltpu.VMEM((4, 128, 128), BF16),
            pltpu.VMEM((128, 128), BF16),
            pltpu.VMEM((32, 16, 256), BF16),
            dma,
            dma,
            dma,
            dma,
            dma,
            dma,
            dma,
            dma((4,)),
            dma((4,)),
            dma,
            dma,
            dma,
            dma,
            pltpu.SemaphoreType.REGULAR,
        ],
        compiler_params=pltpu.CompilerParams(
            collective_id=0, has_side_effects=True, vmem_limit_bytes=40 * 1024 * 1024
        ),
        name="pair_kernel",
    )(
        templ_pair[0],
        main_pair.reshape(2, 32, 16, 128),
        coverage.T,
        pair_mask,
        tri_gain.reshape(1, 64),
        w_project,
        w_bias.T,
        w_tri_out,
        merge_gain.reshape(1, 64),
        w_merge_q.T,
        w_merge_kv,
    )
    return pl.pallas_call(
        out_kernel,
        out_shape=(
            jax.ShapeDtypeStruct((1, 64, 16, 64), BF16),
            jax.ShapeDtypeStruct((64, 16, 128), BF16),
        ),
        in_specs=[vmem] * 3,
        out_specs=(vmem, vmem),
        compiler_params=pltpu.CompilerParams(vmem_limit_bytes=40 * 1024 * 1024),
        name="out_kernel",
    )(new, merged, w_merge_out)


def solution(mesh):
    whole = P()
    tiles = P("tmpl", "row", "col", None)
    pairs = P("row", "col", None)
    return jax.shard_map(
        on_device,
        mesh=mesh,
        in_specs=(tiles, pairs) + (whole,) * 10,
        out_specs=(tiles, pairs),
        check_vma=False,
    )
```

time: 192 us -> 53.7 us (0.28)
  waiting for transfers between devices: 93.3 us -> 0 us
  Pallas kernels: 0 us -> 47.1 us
  local copies, waits for them, and re-layouts: 43.7 us -> 5.5 us
  between operations: 14.5 us -> 0.7 us
  matrix products: 12.3 us -> 0 us
  blocking collectives: 11 us -> 0 us
  starting transfers between devices: 9.38 us -> 0 us
  other arithmetic: 7.53 us -> 0 us
    all_gather x2 -> x0, waiting for transfers between devices: 90.2 us -> none  [the longest x1 69.8 us: on_device(): norm_piece = lax.all_gather(normed, 'col', axis=1, tiled=True)]
    pallas_call x0 -> x2, Pallas kernels: none -> 47.1 us  [the longest x1 46.1 us: on_device(): pl.pallas_call(pair_kernel, out_shape=(piece, piece), in_specs=[anywhere,...]
    slice x5 -> x0, local copies, waits for them, and re-layouts: 13.4 us -> none  [the longest x2 7.73 us: one_group(): key_value[..., hidden:].reshape(group, piece_width, head_count, head_dim)]
    dot_general x9 -> x0, matrix products: 12.3 us -> none  [the longest x1 4.64 us: one_group(): jnp.einsum('ijhk,ikhd->ijhd', weights.astype(jnp.bfloat16), value_part, p...]
    all_gather x1 -> x0, blocking collectives: 11 us -> none  [on_device(): bias_column = lax.all_gather(bias_tile, 'row', axis=1, tiled=True)]
    all_to_all x1 -> x0, starting transfers between devices: 9.3 us -> none  [on_device(): lax.all_to_all(bias_column, 'col', split_axis=1, concat_axis=2, tiled=True)]
    all_gather x2 -> x0, local copies, waits for them, and re-layouts: 7.2 us -> none  [the longest x1 6.99 us: on_device(): norm_piece = lax.all_gather(normed, 'col', axis=1, tiled=True)]
    div x6 -> x0, local copies, waits for them, and re-layouts: 4.35 us -> none  [the longest x1 2.2 us: on_device(): attended = result[2] / result[1][..., None]]
  transfers between devices with their start and end apart: 3 -> 0, of which waited for: 3 -> 0; matrix products, arithmetic and copies ran while one was open for 7% -> 0% of each run, Pallas kernels for 0% -> 0%
where the time goes in v1:
time: 53.7 us; the launch traced here: 53.3 us
  Pallas kernels  47.1 us (88%)
  local copies, waits for them, and re-layouts  5.5 us (10%)
  between operations  0.7 us (1%)
    pallas_call x1, Pallas kernels, on_device(): pl.pallas_call(pair_kernel, out_shape=(piece, piece), in_specs=[anywhere,...  46.1 us
    unnamed x24, local copies, waits for them, and re-layouts  5.5 us

profile of v1, /device:TPU:1, one launch (start us, length us, event | category | flops | bytes accessed | tf_op | source)
XLA Modules:
  0.0 53.3 jit_solution(17150306883210286951)
XLA Ops:
  0.6 0.0 copy-start.11
  0.6 0.0 copy-start.8
  0.7 0.0 copy-start.9
  0.7 0.0 copy-start.7
  0.7 0.0 copy-start.10
  0.7 0.6 %copy-done.11 = f32[64]{0:T(128)S(1)} copy-done((f32[64]{0:T(128)S(1)}, f32[64]{0:T(128)}, u32[]{:S(2)}) %copy-start.11) | copy-done | bytes 280
  1.3 0.0 copy-done.8
  1.3 0.0 copy-done.9
  1.3 0.0 copy-done.7
  1.4 0.0 copy-done.10
  1.4 0.0 copy-start
  1.4 0.9 %copy-done = bf16[1,64,16,64]{3,2,1,0:T(8,128)(2,1)S(1)} copy-done((bf16[1,64,16,64]{3,2,1,0:T(8,128)(2,1)S(1)}, bf16[1,64,16,64]{3,2,1,0:T(8,128)(2,1)}, u32[]{:S(2)}) %copy-start) | copy-done | bytes 131096
  2.3 0.0 copy-start.1
  2.3 0.9 %copy-done.1 = bf16[64,16,128]{2,1,0:T(8,128)(2,1)S(1)} copy-done((bf16[64,16,128]{2,1,0:T(8,128)(2,1)S(1)}, bf16[64,16,128]{2,1,0:T(8,128)(2,1)}, u32[]{:S(2)}) %copy-start.1) | copy-done | bytes 262168
  3.3 0.0 copy-start.2
  3.3 0.8 %copy-done.2 = bf16[64,256]{1,0:T(8,128)(2,1)S(1)} copy-done((bf16[64,256]{1,0:T(8,128)(2,1)S(1)}, bf16[64,256]{1,0:T(8,128)(2,1)}, u32[]{:S(2)}) %copy-start.2) | copy-done | bytes 32792
  4.0 0.0 copy-start.3
  4.0 0.7 %copy-done.3 = bf16[64,64]{1,0:T(8,128)(2,1)S(1)} copy-done((bf16[64,64]{1,0:T(8,128)(2,1)S(1)}, bf16[64,64]{1,0:T(8,128)(2,1)}, u32[]{:S(2)}) %copy-start.3) | copy-done | bytes 8216
  4.7 0.0 copy-start.4
  4.7 0.7 %copy-done.4 = bf16[128,64]{0,1:T(8,128)(2,1)S(1)} copy-done((bf16[128,64]{0,1:T(8,128)(2,1)S(1)}, bf16[128,64]{0,1:T(8,128)(2,1)}, u32[]{:S(2)}) %copy-start.4) | copy-done | bytes 16408
  5.5 0.0 copy-start.5
  5.5 0.7 %copy-done.5 = bf16[64,128]{1,0:T(8,128)(2,1)S(1)} copy-done((bf16[64,128]{1,0:T(8,128)(2,1)S(1)}, bf16[64,128]{1,0:T(8,128)(2,1)}, u32[]{:S(2)}) %copy-start.5) | copy-done | bytes 16408
  6.2 0.0 copy-start.6
  6.2 46.1 %pair_kernel.1 = (bf16[32,16,128]{2,1,0:T(8,128)(2,1)S(1)}, bf16[32,16,128]{2,1,0:T(8,128)(2,1)S(1)}) custom-call(bf16[64,16,64]{2,1,0:T(8,128)(2,1)S(1)} %bitcast.7, bf16[2,32,16,128]{3,2,1,0:T(8,128)(2,1)S(1)} %bitcast.8, s32[2,4]{1,0:T(2,128)S(1)} %bitcast.10, s32[2,2]{1,0:T(2,128)S(1)} %copy-done.8, f32[1,64]{1,0:T(1,128)S(1)} %bitcast.12, ...), custom_call_target="tpu_custom_call" | custom-call | tf_op jit(solution)/shard_map/pair_kernel/pallas_call | solution.py:452
  52.3 0.0 copy-done.6
  52.3 1.0 %out_kernel.1 = (bf16[1,64,16,64]{3,2,1,0:T(8,128)(2,1)}, bf16[64,16,128]{2,1,0:T(8,128)(2,1)}) custom-call(bf16[32,16,128]{2,1,0:T(8,128)(2,1)S(1)} %get-tuple-element.4.new_ref, bf16[32,16,128]{2,1,0:T(8,128)(2,1)S(1)} %get-tuple-element.5.merged_ref, bf16[64,128]{1,0:T(8,128)(2,1)S(1)} %copy-done.6), custom_call_target="tpu_custom_call" | custom-call | tf_op jit(solution)/shard_map/out_kernel/pallas_call | solution.py:502
Async XLA Ops:
  0.6 0.7 %copy-start.11 = (f32[64]{0:T(128)S(1)}, f32[64]{0:T(128)}, u32[]{:S(2)}) copy-start(f32[64]{0:T(128)} %param.20) | copy-start | bytes 772
  0.6 0.7 %copy-start.8 = (s32[2,2]{1,0:T(2,128)S(1)}, s32[2,2]{1,0:T(2,128)}, u32[]{:S(2)}) copy-start(s32[2,2]{1,0:T(2,128)} %mask_ref.1) | copy-start | bytes 52
  0.7 0.7 %copy-start.9 = (bf16[64,4]{0,1:T(4,128)(2,1)S(1)}, bf16[64,4]{0,1:T(4,128)(2,1)}, u32[]{:S(2)}) copy-start(bf16[64,4]{0,1:T(4,128)(2,1)} %param.18) | copy-start | bytes 1540
  0.7 0.7 %copy-start.7 = (s32[4,2]{0,1:T(2,128)S(1)}, s32[4,2]{0,1:T(2,128)}, u32[]{:S(2)}) copy-start(s32[4,2]{0,1:T(2,128)} %param.14) | copy-start | bytes 100
  0.7 0.7 %copy-start.10 = (f32[64]{0:T(128)S(1)}, f32[64]{0:T(128)}, u32[]{:S(2)}) copy-start(f32[64]{0:T(128)} %param.16) | copy-start | bytes 772
  1.4 1.0 %copy-start = (bf16[1,64,16,64]{3,2,1,0:T(8,128)(2,1)S(1)}, bf16[1,64,16,64]{3,2,1,0:T(8,128)(2,1)}, u32[]{:S(2)}) copy-start(bf16[1,64,16,64]{3,2,1,0:T(8,128)(2,1)} %param.12) | copy-start | bytes 393220
  2.3 0.9 %copy-start.1 = (bf16[64,16,128]{2,1,0:T(8,128)(2,1)S(1)}, bf16[64,16,128]{2,1,0:T(8,128)(2,1)}, u32[]{:S(2)}) copy-start(bf16[64,16,128]{2,1,0:T(8,128)(2,1)} %param.13) | copy-start | bytes 786436
  3.3 0.8 %copy-start.2 = (bf16[64,256]{1,0:T(8,128)(2,1)S(1)}, bf16[64,256]{1,0:T(8,128)(2,1)}, u32[]{:S(2)}) copy-start(bf16[64,256]{1,0:T(8,128)(2,1)} %w_project_ref.1) | copy-start | bytes 98308
  4.0 0.7 %copy-start.3 = (bf16[64,64]{1,0:T(8,128)(2,1)S(1)}, bf16[64,64]{1,0:T(8,128)(2,1)}, u32[]{:S(2)}) copy-start(bf16[64,64]{1,0:T(8,128)(2,1)} %w_tri_ref.1) | copy-start | bytes 24580
  4.7 0.7 %copy-start.4 = (bf16[128,64]{0,1:T(8,128)(2,1)S(1)}, bf16[128,64]{0,1:T(8,128)(2,1)}, u32[]{:S(2)}) copy-start(bf16[128,64]{0,1:T(8,128)(2,1)} %param.21) | copy-start | bytes 49156
  5.5 0.7 %copy-start.5 = (bf16[64,128]{1,0:T(8,128)(2,1)S(1)}, bf16[64,128]{1,0:T(8,128)(2,1)}, u32[]{:S(2)}) copy-start(bf16[64,128]{1,0:T(8,128)(2,1)} %w_kv_ref.1) | copy-start | bytes 49156
  6.2 46.2 %copy-start.6 = (bf16[64,128]{1,0:T(8,128)(2,1)S(1)}, bf16[64,128]{1,0:T(8,128)(2,1)}, u32[]{:S(2)}) copy-start(bf16[64,128]{1,0:T(8,128)(2,1)} %w_out_ref.1) | copy-start | bytes 49156

commit v2 on v1

v2 whole, which is shorter than its diff:
```python
import jax
import jax.numpy as jnp
from jax import lax
from jax.experimental import pallas as pl
from jax.experimental.pallas import tpu as pltpu
from jax.sharding import PartitionSpec as P

MASK_SHIFT = 10000.0
EPSILON = 1e-05
MESH = pl.DeviceIdType.MESH
F32 = jnp.float32
BF16 = jnp.bfloat16


def iota(shape, axis):
    return lax.broadcasted_iota(jnp.int32, shape, axis)


def dot_nn(a, b):
    return lax.dot_general(a, b, (((1,), (0,)), ((), ())), preferred_element_type=F32)


def dot_nt(a, b):
    return lax.dot_general(a, b, (((1,), (1,)), ((), ())), preferred_element_type=F32)


def dot_tn(a, b):
    return lax.dot_general(a, b, (((0,), (0,)), ((), ())), preferred_element_type=F32)


def split_dot(values, weights):
    high = values.astype(BF16)
    low = (values - high.astype(F32)).astype(BF16)
    return dot_nn(high, weights) + dot_nn(low, weights)


def pair_norm(values, averager, gain):
    center = values.astype(F32) - dot_nn(values, averager)
    spread = split_dot(center * center, averager)
    return (center * lax.rsqrt(spread + EPSILON) * gain).astype(BF16)


def ones_where(condition):
    return jnp.where(condition, 1.0, 0.0).astype(BF16)


def diagonal(doubled):
    both = jnp.concatenate([doubled, doubled], axis=0)
    keep = (iota((128, 128), 0) < 64) == (iota((128, 128), 1) < 64)
    return jnp.where(keep, both, 0.0).astype(BF16)


def pick_columns(width, first):
    return ones_where(iota((width, 128), 0) == first + iota((width, 128), 1) % 64)


def pair_kernel(
    templ_hbm,
    main_hbm,
    coverage_hbm,
    mask_hbm,
    tri_gain_hbm,
    w_project_hbm,
    w_bias_hbm,
    w_tri_hbm,
    merge_gain_hbm,
    w_query_hbm,
    w_kv_hbm,
    new_out,
    merged_out,
    tile,
    coverage_ref,
    mask_ref,
    tri_gain_ref,
    w_project_ref,
    w_bias_ref,
    w_tri_ref,
    merge_gain_ref,
    w_query_ref,
    w_kv_ref,
    packed,
    rows_in,
    bias_rows,
    bias_in,
    bias_full,
    main_in,
    normed,
    keys,
    values,
    queries,
    gates,
    scores,
    gated,
    fresh,
    peers_in,
    merged,
    sizes,
    load_sem,
    rows_send,
    rows_recv,
    cross_send,
    cross_recv,
    bias_send,
    bias_recv,
    main_send,
    main_recv,
    peer_send,
    peer_recv,
    new_send,
    new_recv,
    merged_send,
    merged_recv,
    second_sem,
):
    templ = lax.axis_index("tmpl")
    row = lax.axis_index("row")
    col = lax.axis_index("col")
    plane = col // 2
    half, chunk = col // 8, col % 8
    own_cols = pl.ds(pl.multiple_of(16 * col, 16), 16)

    loads = [
        pltpu.make_async_copy(source, target, load_sem.at[index])
        for index, (source, target) in enumerate(
            (
                (templ_hbm, tile),
                (tri_gain_hbm, tri_gain_ref),
                (w_bias_hbm, w_bias_ref),
                (w_project_hbm, w_project_ref),
                (w_tri_hbm, w_tri_ref),
                (merge_gain_hbm, merge_gain_ref),
                (w_query_hbm, w_query_ref),
                (w_kv_hbm, w_kv_ref),
                (coverage_hbm, coverage_ref),
                (mask_hbm, mask_ref),
            )
        )
    ]
    barrier = pltpu.get_barrier_semaphore()
    for step in range(1, 16):
        pl.semaphore_signal(barrier, inc=1, device_id=(templ, row, (col + step) % 16), device_id_type=MESH)
    for step in range(1, 4):
        pl.semaphore_signal(barrier, inc=1, device_id=(templ, (row + step) % 4, col), device_id_type=MESH)
        pl.semaphore_signal(barrier, inc=1, device_id=((templ + step) % 4, row, col), device_id_type=MESH)
    for load in loads:
        load.start()

    for load in loads[:3]:
        load.wait()
    eye = iota((64, 128), 0)
    lane = iota((64, 128), 1)
    low_rows = tile[pl.ds(0, 32)].reshape(512, 64)
    high_rows = tile[pl.ds(32, 32)].reshape(512, 64)
    together = dot_nn(low_rows, ones_where(eye == lane)) + dot_nn(high_rows, ones_where(eye + 64 == lane))
    packed[...] = together.astype(BF16).reshape(32, 16, 128)

    averager = jnp.where(
        (iota((128, 128), 0) < 64) == (iota((128, 128), 1) < 64), 1.0 / 64, 0.0
    ).astype(BF16)
    tri_gain = jnp.concatenate([tri_gain_ref[...], tri_gain_ref[...]], axis=1)

    pl.semaphore_wait(barrier, 21)
    for step in range(1, 4):
        pl.semaphore_signal(second_sem, inc=1, device_id=((templ + step) % 4, row, col), device_id_type=MESH)

    def far_first(index):
        away = (index // 2 + 1) // 2 * (2 * (index // 2 % 2) - 1)
        return 2 * ((plane + 4 + away) % 8) + (col + index) % 2

    def send_to_columns(source_of, target, local_target, send_sem, recv_sem):
        def one(index, carry):
            to = far_first(index)
            pltpu.make_async_remote_copy(
                src_ref=source_of(to),
                dst_ref=target,
                send_sem=send_sem,
                recv_sem=recv_sem,
                device_id=(templ, row, to),
                device_id_type=MESH,
            ).start()
            return carry

        lax.fori_loop(0, 14, one, 0)
        one(15, 0)
        pltpu.make_async_copy(source_of(col), local_target, recv_sem).start()

    rows_place = rows_in.at[:, own_cols, :]
    send_to_columns(
        lambda to: packed.at[pl.ds(4 * (to % 8), 4)], rows_place, rows_place, rows_send, rows_recv
    )

    own_normed = pair_norm(packed[...].reshape(512, 128), averager, tri_gain)
    w_bias = dot_nn(w_bias_ref[...], pick_columns(64, 0))
    which = iota((256, 128), 0)
    spread_bias = jnp.zeros((256, 128), F32)
    for head in range(4):
        spread_bias = jnp.where(which // 64 == head, w_bias[head : head + 1, :], spread_bias)
    spread_bias = jnp.where((which // 32) % 2 == iota((256, 128), 1) // 64, spread_bias, 0.0).astype(BF16)
    every_bias = dot_nt(own_normed, spread_bias).reshape(32, 16, 256)
    place = iota((16, 256), 1) % 32
    chosen = jnp.zeros((16, 256), F32)
    for index in range(32):
        chosen = jnp.where(place == index, every_bias[index], chosen)
    chosen = chosen.astype(BF16)
    bias_rows[0, row] = chosen[:, :128]
    bias_rows[1, row] = chosen[:, 128:]

    for step in range(1, 4):
        pltpu.make_async_remote_copy(
            src_ref=bias_rows.at[:, row],
            dst_ref=bias_rows.at[:, row],
            send_sem=cross_send,
            recv_sem=cross_recv,
            device_id=(templ, (row + step) % 4, col),
            device_id_type=MESH,
        ).start()

    for load in loads[3:]:
        load.wait()
    w_project = w_project_ref[...]
    double = pick_columns(64, 0)

    def turned(first):
        columns = ones_where(iota((128, 256), 1) == first + iota((128, 256), 0) % 64)
        wide = dot_nn(dot_nt(columns, w_project).astype(BF16), double)
        keep = (iota((128, 128), 0) < 64) == (iota((128, 128), 1) < 64)
        return jnp.where(keep, wide, 0.0).astype(BF16)

    turned_query, turned_value, turned_gate = turned(0), turned(128), turned(192)
    w_key = diagonal(dot_nn(w_project, pick_columns(256, 64)))
    w_tri = diagonal(dot_nn(w_tri_ref[...], double))
    ones_rows = jnp.ones((16, 256), BF16)
    head_of = iota((128, 128), 0) // 16

    w_query = w_query_ref[...]
    nothing = jnp.zeros_like(w_query)
    w_kv = w_kv_ref[...]
    w_merge_key = diagonal(dot_nn(w_kv, pick_columns(128, 0)))
    w_merge_value = diagonal(dot_nn(w_kv, pick_columns(128, 64)))
    merge_gain = jnp.concatenate([merge_gain_ref[...], merge_gain_ref[...]], axis=1)
    summer = ones_where(iota((128, 128), 0) // 16 == iota((128, 128), 1) // 16)

    def drain(ref, sem):
        pltpu.make_async_copy(ref, ref, sem).wait()

    drain(sizes.at[pl.ds(0, 3)], cross_recv)
    for heads in range(2):
        bias_place = bias_in.at[heads, :, own_cols, :]
        send_to_columns(
            lambda to, heads=heads: bias_rows.at[heads, pl.ds(2 * (to // 8), 2)],
            bias_place,
            bias_place,
            bias_send.at[heads],
            bias_recv.at[heads],
        )

    main_place = main_in.at[:, pl.ds(pl.multiple_of(16 * chunk, 16), 16), :]
    pltpu.make_async_copy(main_hbm.at[:, 4 * chunk + templ], main_place, main_recv).start()

    def send_main(step, carry):
        to_chunk = (chunk + step) % 8
        pltpu.make_async_remote_copy(
            src_ref=main_hbm.at[:, 4 * to_chunk + templ],
            dst_ref=main_place,
            send_sem=main_send,
            recv_sem=main_recv,
            device_id=(templ, row, 8 * half + to_chunk),
            device_id_type=MESH,
        ).start()
        return carry

    lax.fori_loop(1, 8, send_main, 0)

    row_block = row // 2
    cover_row = coverage_ref[row_block, templ]
    shift_low = MASK_SHIFT * ((cover_row * coverage_ref[0, templ] * mask_ref[row_block, 0]).astype(F32) - 1.0)
    shift_high = MASK_SHIFT * ((cover_row * coverage_ref[1, templ] * mask_ref[row_block, 1]).astype(F32) - 1.0)
    gap = shift_high - shift_low
    mine = pl.ds(pl.multiple_of(128 * half, 128), 128)

    drain(rows_in, rows_recv)
    every_normed = pair_norm(rows_in[...].reshape(1024, 128), averager, tri_gain)
    normed[...] = every_normed.reshape(4, 256, 128)
    keys[...] = dot_nn(every_normed, w_key).astype(BF16).reshape(4, 256, 128)
    every_value = dot_nt(turned_value, every_normed).astype(BF16)
    own_part = normed[:, mine, :].reshape(512, 128)
    every_query = (dot_nt(turned_query, own_part) * 0.25).astype(BF16)
    every_gate = jax.nn.sigmoid(dot_nt(turned_gate, own_part))
    for pair in range(4):
        values[pair] = every_value[:, 256 * pair : 256 * pair + 256]
        queries[pair] = every_query[:, 128 * pair : 128 * pair + 128]
        gates[pair] = every_gate[:, 128 * pair : 128 * pair + 128]

    def score(pair, carry):
        pair_keys, pair_queries = keys[pair], queries[pair]
        nothing = jnp.zeros_like(pair_queries)
        for index in range(4):
            two_heads = jnp.concatenate(
                [
                    jnp.where(head_of == 2 * index, pair_queries, nothing),
                    jnp.where(head_of == 2 * index + 1, pair_queries, nothing),
                ],
                axis=1,
            )
            scores[pair, index] = dot_nn(pair_keys, two_heads)
        return carry

    lax.fori_loop(0, 4, score, 0)

    def soft(values, bias):
        values = values + bias
        low, high = values[:128], values[128:]
        top_low = jnp.max(low, axis=0, keepdims=True)
        top_high = jnp.max(high, axis=0, keepdims=True)
        return jnp.concatenate(
            [
                jnp.exp(low - jnp.maximum(top_low, top_high + gap)),
                jnp.exp(high - jnp.maximum(top_low - gap, top_high)),
            ],
            axis=0,
        ).astype(BF16)

    def pair_of(step):
        return templ ^ (3 - step ^ (1 - step // 2))

    def finish(step):
        pair = pair_of(step)
        projected = dot_tn(gated[pair], w_tri)
        result = (rows_in[pair, mine, :].astype(F32) + projected).astype(BF16)
        fresh[pair] = result

        @pl.when(step == 3)
        def _():
            peers_in[templ] = result

        @pl.when(step < 3)
        def _():
            pltpu.make_async_remote_copy(
                src_ref=fresh.at[pair],
                dst_ref=peers_in.at[templ],
                send_sem=peer_send.at[step],
                recv_sem=peer_recv.at[templ],
                device_id=(pair, row, col),
                device_id_type=MESH,
            ).start()

    def attend(count, carry):
        heads, turn = count // 2, count % 2

        @pl.when(turn == 0)
        def _():
            drain(bias_in.at[heads], bias_recv.at[heads])
            first_half = iota((256, 128), 1) < 64
            one = bias_in[heads, 0].astype(F32)
            two = bias_in[heads, 1].astype(F32)
            bias_full[0] = jnp.where(first_half, one, pltpu.roll(two, 64, 1))
            bias_full[1] = jnp.where(first_half, pltpu.roll(one, 64, 1), two)

        for step in (2 * turn, 2 * turn + 1):
            pair = pair_of(step)
            for side in range(2):
                both = scores[pair, 2 * side + heads]
                weights = jnp.concatenate(
                    [soft(both[:, :128], bias_full[0]), soft(both[:, 128:], bias_full[1])], axis=1
                )
                place = pl.ds(pl.multiple_of(64 * side + 32 * heads, 32), 32)
                mixed = dot_nn(jnp.concatenate([values[pair, place, :], ones_rows], axis=0), weights)
                attended = jnp.concatenate(
                    [mixed[:16, :128] / mixed[32:, :128], mixed[16:32, 128:] / mixed[32:, 128:]], axis=0
                )
                gated[pair, place, :] = (attended * gates[pair, place, :]).astype(BF16)

        @pl.when(heads == 1)
        def _():
            finish(2 * turn)
            finish(2 * turn + 1)

        return carry

    lax.fori_loop(0, 4, attend, 0)

    new_place = new_out.at[pl.ds(4 * chunk, 4)]

    def returned(to_chunk):
        return fresh.at[:, pl.ds(pl.multiple_of(16 * to_chunk, 16), 16), :]

    def send_new(step, carry):
        to_chunk = (chunk + step) % 8
        pltpu.make_async_remote_copy(
            src_ref=returned(to_chunk),
            dst_ref=new_place,
            send_sem=new_send,
            recv_sem=new_recv,
            device_id=(templ, row, 8 * half + to_chunk),
            device_id_type=MESH,
        ).start()
        return carry

    lax.fori_loop(1, 8, send_new, 0)
    pltpu.make_async_copy(returned(chunk), new_place, new_recv).start()

    pltpu.make_async_copy(main_in, main_in, main_recv).wait()
    main_query = 0.25 * (
        dot_nt(main_in[0], jnp.concatenate([w_query, nothing], axis=0))
        + dot_nt(main_in[1], jnp.concatenate([nothing, w_query], axis=0))
    )

    def wait_peer(step, carry):
        source = (templ + step) % 4
        pltpu.make_async_copy(peers_in.at[source], peers_in.at[source], peer_recv.at[source]).wait()
        return carry

    lax.fori_loop(1, 4, wait_peer, 0)
    peers_normed = pair_norm(peers_in[...].reshape(512, 128), averager, merge_gain)
    merge_keys = dot_nn(peers_normed, w_merge_key).astype(BF16).astype(F32).reshape(4, 128, 128)
    shown = dot_nn(peers_normed, w_merge_value).astype(BF16).astype(F32).reshape(4, 128, 128)
    products = split_dot((main_query[None] * merge_keys).reshape(512, 128), summer).reshape(4, 128, 128)
    merge_scores = []
    for other in range(4):
        valid = coverage_ref[row_block, other] * coverage_ref[half, other] * mask_ref[row_block, half]
        merge_scores.append(products[other] + MASK_SHIFT * (valid.astype(F32) - 1.0))
    highest = jnp.maximum(
        jnp.maximum(merge_scores[0], merge_scores[1]), jnp.maximum(merge_scores[2], merge_scores[3])
    )
    weights = [jnp.exp(one - highest) for one in merge_scores]
    total = (weights[0] + weights[1]) + (weights[2] + weights[3])
    blend = (weights[0] * shown[0] + weights[1] * shown[1]) + (weights[2] * shown[2] + weights[3] * shown[3])
    merged[...] = (blend / total).astype(BF16)

    pltpu.make_async_copy(
        merged.at[pl.ds(pl.multiple_of(16 * chunk, 16), 16), :],
        merged_out.at[4 * chunk + templ],
        merged_recv,
    ).start()

    pl.semaphore_wait(second_sem, 3)

    def send_merged(step, carry):
        to_templ, to_chunk = templ ^ (3 - step % 4), (chunk + 3 + step // 4) % 8

        @pl.when((to_templ != templ) | (to_chunk != chunk))
        def _():
            pltpu.make_async_remote_copy(
                src_ref=merged.at[pl.ds(pl.multiple_of(16 * to_chunk, 16), 16), :],
                dst_ref=merged_out.at[4 * chunk + templ],
                send_sem=merged_send,
                recv_sem=merged_recv,
                device_id=(to_templ, row, 8 * half + to_chunk),
                device_id_type=MESH,
            ).start()

        return carry

    lax.fori_loop(0, 32, send_merged, 0)

    for step in range(3):
        drain(fresh.at[0], peer_send.at[step])
    drain(sizes.at[pl.ds(0, 30)], rows_send)
    drain(sizes.at[pl.ds(0, 3)], cross_send)
    for heads in range(2):
        drain(sizes.at[pl.ds(0, 15)], bias_send.at[heads])
    drain(sizes.at[pl.ds(0, 7)], main_send)
    drain(sizes.at[pl.ds(0, 14)], new_send)
    drain(packed.at[pl.ds(0, 31)], merged_send)
    drain(new_out, new_recv)
    drain(merged_out, merged_recv)


def out_kernel(new_ref, merged_ref, w_out_ref, templ_ref, embedding_ref):
    new = new_ref[...]
    templ_ref[0, pl.ds(0, 32)] = new[:, :, :64]
    templ_ref[0, pl.ds(32, 32)] = new[:, :, 64:]
    merged = merged_ref[...].reshape(512, 128)
    w_out = w_out_ref[...]
    nothing = jnp.zeros_like(w_out)
    first = dot_nn(merged, jnp.concatenate([w_out, nothing], axis=0))
    second = dot_nn(merged, jnp.concatenate([nothing, w_out], axis=0))
    embedding_ref[pl.ds(0, 32)] = first.astype(BF16).reshape(32, 16, 128)
    embedding_ref[pl.ds(32, 32)] = second.astype(BF16).reshape(32, 16, 128)


def on_device(
    templ_pair,
    main_pair,
    coverage,
    pair_mask,
    tri_gain,
    w_project,
    w_bias,
    w_tri_out,
    merge_gain,
    w_merge_q,
    w_merge_kv,
    w_merge_out,
):
    vmem = pl.BlockSpec(memory_space=pltpu.VMEM)
    anywhere = pl.BlockSpec(memory_space=pl.ANY)
    piece = jax.ShapeDtypeStruct((32, 16, 128), BF16)
    dma = pltpu.SemaphoreType.DMA
    new, merged = pl.pallas_call(
        pair_kernel,
        out_shape=(piece, piece),
        in_specs=[pl.BlockSpec(memory_space=pltpu.HBM)] * 11,
        out_specs=(anywhere, anywhere),
        scratch_shapes=[
            pltpu.VMEM((64, 16, 64), BF16),
            pltpu.SMEM((2, 4), jnp.int32),
            pltpu.SMEM((2, 2), jnp.int32),
            pltpu.VMEM((1, 64), F32),
            pltpu.VMEM((64, 256), BF16),
            pltpu.VMEM((4, 64), BF16),
            pltpu.VMEM((64, 64), BF16),
            pltpu.VMEM((1, 64), F32),
            pltpu.VMEM((64, 128), BF16),
            pltpu.VMEM((64, 128), BF16),
            pltpu.VMEM((32, 16, 128), BF16),
            pltpu.VMEM((4, 256, 128), BF16),
            pltpu.VMEM((2, 4, 16, 128), BF16),
            pltpu.VMEM((2, 2, 256, 128), BF16),
            pltpu.VMEM((2, 256, 128), F32),
            pltpu.VMEM((2, 128, 128), BF16),
            pltpu.VMEM((4, 256, 128), BF16),
            pltpu.VMEM((4, 256, 128), BF16),
            pltpu.VMEM((4, 128, 256), BF16),
            pltpu.VMEM((4, 128, 128), BF16),
            pltpu.VMEM((4, 128, 128), F32),
            pltpu.VMEM((4, 4, 256, 256), F32),
            pltpu.VMEM((4, 128, 128), BF16),
            pltpu.VMEM((4, 128, 128), BF16),
            pltpu.VMEM((4, 128, 128), BF16),
            pltpu.VMEM((128, 128), BF16),
            pltpu.VMEM((32, 16, 256), BF16),
            dma((10,)),
            dma,
            dma,
            dma,
            dma,
            dma((2,)),
            dma((2,)),
            dma,
            dma,
            dma((4,)),
            dma((4,)),
            dma,
            dma,
            dma,
            dma,
            pltpu.SemaphoreType.REGULAR,
        ],
        compiler_params=pltpu.CompilerParams(
            collective_id=0, has_side_effects=True, vmem_limit_bytes=64 * 1024 * 1024
        ),
        name="pair_kernel",
    )(
        templ_pair[0],
        main_pair.reshape(2, 32, 16, 128),
        coverage.T,
        pair_mask,
        tri_gain.reshape(1, 64),
        w_project,
        w_bias.T,
        w_tri_out,
        merge_gain.reshape(1, 64),
        w_merge_q.T,
        w_merge_kv,
    )
    return pl.pallas_call(
        out_kernel,
        out_shape=(
            jax.ShapeDtypeStruct((1, 64, 16, 64), BF16),
            jax.ShapeDtypeStruct((64, 16, 128), BF16),
        ),
        in_specs=[vmem] * 3,
        out_specs=(vmem, vmem),
        compiler_params=pltpu.CompilerParams(vmem_limit_bytes=64 * 1024 * 1024),
        name="out_kernel",
    )(new, merged, w_merge_out)


def solution(mesh):
    whole = P()
    tiles = P("tmpl", "row", "col", None)
    pairs = P("row", "col", None)
    return jax.shard_map(
        on_device,
        mesh=mesh,
        in_specs=(tiles, pairs) + (whole,) * 10,
        out_specs=(tiles, pairs),
        check_vma=False,
    )
```

time: 53.7 us -> 38.2 us (0.71)
  Pallas kernels: 47.1 us -> 37.4 us
  local copies, waits for them, and re-layouts: 5.5 us -> 0 us
    pallas_call x1, Pallas kernels: 46.1 us -> 35.5 us  [on_device(): pl.pallas_call(pair_kernel, out_shape=(piece, piece), in_specs=[pl.BlockS...]
    unnamed x24 -> x0, local copies, waits for them, and re-layouts: 5.5 us -> none
    pallas_call x1, Pallas kernels: 0.97 us -> 1.94 us  [on_device(): pl.pallas_call(out_kernel, out_shape=(jax.ShapeDtypeStruct((1, 64, 16, 64...]
where the time goes in v2:
time: 38.2 us; the launch traced here: 38.1 us
  Pallas kernels  37.4 us (98%)
  between operations  0.64 us (2%)
    pallas_call x1, Pallas kernels, on_device(): pl.pallas_call(pair_kernel, out_shape=(piece, piece), in_specs=[pl.BlockS...  35.5 us
    pallas_call x1, Pallas kernels, on_device(): pl.pallas_call(out_kernel, out_shape=(jax.ShapeDtypeStruct((1, 64, 16, 64...  1.94 us

profile of v2, /device:TPU:1, one launch (start us, length us, event | category | flops | bytes accessed | tf_op | source)
XLA Modules:
  0.0 38.1 jit_solution(10096718410216931287)
XLA Ops:
  0.6 35.5 %pair_kernel.1 = (bf16[32,16,128]{2,1,0:T(8,128)(2,1)}, bf16[32,16,128]{2,1,0:T(8,128)(2,1)}) custom-call(bf16[64,16,64]{2,1,0:T(8,128)(2,1)} %bitcast.7, bf16[2,32,16,128]{3,2,1,0:T(8,128)(2,1)} %bitcast.8, s32[2,4]{1,0:T(2,128)} %bitcast.10, s32[2,2]{1,0:T(2,128)} %mask_hbm.1, f32[1,64]{1,0:T(1,128)} %bitcast.12, bf16[64,256]{1,0:T(8,128)(2,1)} %w_project_hbm.1, ...), custom_call_target="tpu_custom_call" | custom-call | tf_op jit(solution)/shard_map/pair_kernel/pallas_call | solution.py:500
  36.1 1.9 %out_kernel.1 = (bf16[1,64,16,64]{3,2,1,0:T(8,128)(2,1)}, bf16[64,16,128]{2,1,0:T(8,128)(2,1)}) custom-call(bf16[32,16,128]{2,1,0:T(8,128)(2,1)} %get-tuple-element.4.new_ref, bf16[32,16,128]{2,1,0:T(8,128)(2,1)} %get-tuple-element.5.merged_ref, bf16[64,128]{1,0:T(8,128)(2,1)} %w_out_ref.1), custom_call_target="tpu_custom_call" | custom-call | tf_op jit(solution)/shard_map/out_kernel/pallas_call | solution.py:567

commit v3 on v2

--- a/solution.py
+++ b/solution.py
@@ -159,36 +159,6 @@
     ).astype(BF16)
     tri_gain = jnp.concatenate([tri_gain_ref[...], tri_gain_ref[...]], axis=1)
 
-    pl.semaphore_wait(barrier, 21)
-    for step in range(1, 4):
-        pl.semaphore_signal(second_sem, inc=1, device_id=((templ + step) % 4, row, col), device_id_type=MESH)
-
-    def far_first(index):
-        away = (index // 2 + 1) // 2 * (2 * (index // 2 % 2) - 1)
-        return 2 * ((plane + 4 + away) % 8) + (col + index) % 2
-
-    def send_to_columns(source_of, target, local_target, send_sem, recv_sem):
-        def one(index, carry):
-            to = far_first(index)
-            pltpu.make_async_remote_copy(
-                src_ref=source_of(to),
-                dst_ref=target,
-                send_sem=send_sem,
-                recv_sem=recv_sem,
-                device_id=(templ, row, to),
-                device_id_type=MESH,
-            ).start()
-            return carry
-
-        lax.fori_loop(0, 14, one, 0)
-        one(15, 0)
-        pltpu.make_async_copy(source_of(col), local_target, recv_sem).start()
-
-    rows_place = rows_in.at[:, own_cols, :]
-    send_to_columns(
-        lambda to: packed.at[pl.ds(4 * (to % 8), 4)], rows_place, rows_place, rows_send, rows_recv
-    )
-
     own_normed = pair_norm(packed[...].reshape(512, 128), averager, tri_gain)
     w_bias = dot_nn(w_bias_ref[...], pick_columns(64, 0))
     which = iota((256, 128), 0)
@@ -205,6 +175,36 @@
     bias_rows[0, row] = chosen[:, :128]
     bias_rows[1, row] = chosen[:, 128:]
 
+    pl.semaphore_wait(barrier, 21)
+    for step in range(1, 4):
+        pl.semaphore_signal(second_sem, inc=1, device_id=((templ + step) % 4, row, col), device_id_type=MESH)
+
+    def far_first(index):
+        away = (index // 2 + 1) // 2 * (2 * (index // 2 % 2) - 1)
+        return 2 * ((plane + 4 + away) % 8) + (col + index) % 2
+
+    def send_to_columns(source_of, target, local_target, send_sem, recv_sem):
+        def one(index, carry):
+            to = far_first(index)
+            pltpu.make_async_remote_copy(
+                src_ref=source_of(to),
+                dst_ref=target,
+                send_sem=send_sem,
+                recv_sem=recv_sem,
+                device_id=(templ, row, to),
+                device_id_type=MESH,
+            ).start()
+            return carry
+
+        lax.fori_loop(0, 14, one, 0)
+        one(15, 0)
+        pltpu.make_async_copy(source_of(col), local_target, recv_sem).start()
+
+    rows_place = rows_in.at[:, own_cols, :]
+    send_to_columns(
+        lambda to: packed.at[pl.ds(4 * (to % 8), 4)], rows_place, rows_place, rows_send, rows_recv
+    )
+
     for step in range(1, 4):
         pltpu.make_async_remote_copy(
             src_ref=bias_rows.at[:, row],
@@ -370,10 +370,9 @@
                 )
                 gated[pair, place, :] = (attended * gates[pair, place, :]).astype(BF16)
 
-        @pl.when(heads == 1)
-        def _():
-            finish(2 * turn)
-            finish(2 * turn + 1)
+            @pl.when(heads == 1)
+            def _(step=step):
+                finish(step)
 
         return carry
 

time: 38.2 us -> 38 us (level)
  no operation moved by 1% of the time
where the time goes in v3:
time: 38 us; the launch traced here: 37.9 us
  Pallas kernels  37.2 us (98%)
  between operations  0.64 us (2%)
    pallas_call x1, Pallas kernels, on_device(): pl.pallas_call(pair_kernel, out_shape=(piece, piece), in_specs=[pl.BlockS...  35.3 us
    pallas_call x1, Pallas kernels, on_device(): pl.pallas_call(out_kernel, out_shape=(jax.ShapeDtypeStruct((1, 64, 16, 64...  1.94 us

profile of v3, /device:TPU:1, one launch (start us, length us, event | category | flops | bytes accessed | tf_op | source)
XLA Modules:
  0.0 37.9 jit_solution(15832550657102630366)
XLA Ops:
  0.6 35.3 %pair_kernel.1 = (bf16[32,16,128]{2,1,0:T(8,128)(2,1)}, bf16[32,16,128]{2,1,0:T(8,128)(2,1)}) custom-call(bf16[64,16,64]{2,1,0:T(8,128)(2,1)} %bitcast.7, bf16[2,32,16,128]{3,2,1,0:T(8,128)(2,1)} %bitcast.8, s32[2,4]{1,0:T(2,128)} %bitcast.10, s32[2,2]{1,0:T(2,128)} %mask_hbm.1, f32[1,64]{1,0:T(1,128)} %bitcast.12, bf16[64,256]{1,0:T(8,128)(2,1)} %w_project_hbm.1, ...), custom_call_target="tpu_custom_call" | custom-call | tf_op jit(solution)/shard_map/pair_kernel/pallas_call | solution.py:499
  35.9 1.9 %out_kernel.1 = (bf16[1,64,16,64]{3,2,1,0:T(8,128)(2,1)}, bf16[64,16,128]{2,1,0:T(8,128)(2,1)}) custom-call(bf16[32,16,128]{2,1,0:T(8,128)(2,1)} %get-tuple-element.4.new_ref, bf16[32,16,128]{2,1,0:T(8,128)(2,1)} %get-tuple-element.5.merged_ref, bf16[64,128]{1,0:T(8,128)(2,1)} %w_out_ref.1), custom_call_target="tpu_custom_call" | custom-call | tf_op jit(solution)/shard_map/out_kernel/pallas_call | solution.py:566

commit v4 on v3

--- a/solution.py
+++ b/solution.py
@@ -404,20 +404,25 @@
         + dot_nt(main_in[1], jnp.concatenate([nothing, w_query], axis=0))
     )
 
-    def wait_peer(step, carry):
-        source = (templ + step) % 4
-        pltpu.make_async_copy(peers_in.at[source], peers_in.at[source], peer_recv.at[source]).wait()
-        return carry
-
-    lax.fori_loop(1, 4, wait_peer, 0)
-    peers_normed = pair_norm(peers_in[...].reshape(512, 128), averager, merge_gain)
-    merge_keys = dot_nn(peers_normed, w_merge_key).astype(BF16).astype(F32).reshape(4, 128, 128)
-    shown = dot_nn(peers_normed, w_merge_value).astype(BF16).astype(F32).reshape(4, 128, 128)
-    products = split_dot((main_query[None] * merge_keys).reshape(512, 128), summer).reshape(4, 128, 128)
+    def prepare(first, second):
+        both = jnp.concatenate([peers_in[first], peers_in[second]], axis=0)
+        both_normed = pair_norm(both, averager, merge_gain)
+        merge_keys = dot_nn(both_normed, w_merge_key).astype(BF16).astype(F32)
+        both_shown = dot_nn(both_normed, w_merge_value).astype(BF16).astype(F32)
+        products = split_dot(jnp.concatenate([main_query, main_query], axis=0) * merge_keys, summer)
+        for index, other in enumerate((first, second)):
+            valid = coverage_ref[row_block, other] * coverage_ref[half, other] * mask_ref[row_block, half]
+            part = slice(128 * index, 128 * index + 128)
+            merge_scores.append(products[part] + MASK_SHIFT * (valid.astype(F32) - 1.0))
+            shown.append(both_shown[part])
+
     merge_scores = []
-    for other in range(4):
-        valid = coverage_ref[row_block, other] * coverage_ref[half, other] * mask_ref[row_block, half]
-        merge_scores.append(products[other] + MASK_SHIFT * (valid.astype(F32) - 1.0))
+    shown = []
+    drain(peers_in.at[templ ^ 1], peer_recv.at[templ ^ 1])
+    prepare(templ, templ ^ 1)
+    for other in (templ ^ 2, templ ^ 3):
+        drain(peers_in.at[other], peer_recv.at[other])
+    prepare(templ ^ 2, templ ^ 3)
     highest = jnp.maximum(
         jnp.maximum(merge_scores[0], merge_scores[1]), jnp.maximum(merge_scores[2], merge_scores[3])
     )
@@ -435,7 +440,7 @@
     pl.semaphore_wait(second_sem, 3)
 
     def send_merged(step, carry):
-        to_templ, to_chunk = templ ^ (3 - step % 4), (chunk + 3 + step // 4) % 8
+        to_templ, to_chunk = templ ^ (3 - step // 8), (chunk + 4 + step) % 8
 
         @pl.when((to_templ != templ) | (to_chunk != chunk))
         def _():

time: 38 us -> 37.8 us (level)
  no operation moved by 1% of the time
where the time goes in v4:
time: 37.8 us; the launch traced here: 37.6 us
  Pallas kernels  37 us (98%)
  between operations  0.64 us (2%)
    pallas_call x1, Pallas kernels, on_device(): pl.pallas_call(pair_kernel, out_shape=(piece, piece), in_specs=[pl.BlockS...  35.1 us
    pallas_call x1, Pallas kernels, on_device(): pl.pallas_call(out_kernel, out_shape=(jax.ShapeDtypeStruct((1, 64, 16, 64...  1.94 us

profile of v4, /device:TPU:1, one launch (start us, length us, event | category | flops | bytes accessed | tf_op | source)
XLA Modules:
  0.0 37.6 jit_solution(6686890369416896387)
XLA Ops:
  0.6 35.1 %pair_kernel.1 = (bf16[32,16,128]{2,1,0:T(8,128)(2,1)}, bf16[32,16,128]{2,1,0:T(8,128)(2,1)}) custom-call(bf16[64,16,64]{2,1,0:T(8,128)(2,1)} %bitcast.7, bf16[2,32,16,128]{3,2,1,0:T(8,128)(2,1)} %bitcast.8, s32[2,4]{1,0:T(2,128)} %bitcast.10, s32[2,2]{1,0:T(2,128)} %mask_hbm.1, f32[1,64]{1,0:T(1,128)} %bitcast.12, bf16[64,256]{1,0:T(8,128)(2,1)} %w_project_hbm.1, ...), custom_call_target="tpu_custom_call" | custom-call | tf_op jit(solution)/shard_map/pair_kernel/pallas_call | solution.py:504
  35.7 1.9 %out_kernel.1 = (bf16[1,64,16,64]{3,2,1,0:T(8,128)(2,1)}, bf16[64,16,128]{2,1,0:T(8,128)(2,1)}) custom-call(bf16[32,16,128]{2,1,0:T(8,128)(2,1)} %get-tuple-element.4.new_ref, bf16[32,16,128]{2,1,0:T(8,128)(2,1)} %get-tuple-element.5.merged_ref, bf16[64,128]{1,0:T(8,128)(2,1)} %w_out_ref.1), custom_call_target="tpu_custom_call" | custom-call | tf_op jit(solution)/shard_map/out_kernel/pallas_call | solution.py:571

commit v5 on v4

--- a/solution.py
+++ b/solution.py
@@ -136,13 +136,14 @@
             )
         )
     ]
+    loads[0].start()
     barrier = pltpu.get_barrier_semaphore()
-    for step in range(1, 16):
+    for step in (8, 9, 7, 10, 6, 11, 5, 12, 4, 13, 3, 14, 2, 15, 1):
         pl.semaphore_signal(barrier, inc=1, device_id=(templ, row, (col + step) % 16), device_id_type=MESH)
     for step in range(1, 4):
         pl.semaphore_signal(barrier, inc=1, device_id=(templ, (row + step) % 4, col), device_id_type=MESH)
         pl.semaphore_signal(barrier, inc=1, device_id=((templ + step) % 4, row, col), device_id_type=MESH)
-    for load in loads:
+    for load in loads[1:]:
         load.start()
 
     for load in loads[:3]:

time: 37.8 us -> 37.7 us (level)
  no operation moved by 1% of the time
where the time goes in v5:
time: 37.7 us; the launch traced here: 37.6 us
  Pallas kernels  37 us (98%)
  between operations  0.64 us (2%)
    pallas_call x1, Pallas kernels, on_device(): pl.pallas_call(pair_kernel, out_shape=(piece, piece), in_specs=[pl.BlockS...  35 us
    pallas_call x1, Pallas kernels, on_device(): pl.pallas_call(out_kernel, out_shape=(jax.ShapeDtypeStruct((1, 64, 16, 64...  1.94 us

profile of v5, /device:TPU:1, one launch (start us, length us, event | category | flops | bytes accessed | tf_op | source)
XLA Modules:
  0.0 37.6 jit_solution(13398877355073630865)
XLA Ops:
  0.6 35.0 %pair_kernel.1 = (bf16[32,16,128]{2,1,0:T(8,128)(2,1)}, bf16[32,16,128]{2,1,0:T(8,128)(2,1)}) custom-call(bf16[64,16,64]{2,1,0:T(8,128)(2,1)} %bitcast.7, bf16[2,32,16,128]{3,2,1,0:T(8,128)(2,1)} %bitcast.8, s32[2,4]{1,0:T(2,128)} %bitcast.10, s32[2,2]{1,0:T(2,128)} %mask_hbm.1, f32[1,64]{1,0:T(1,128)} %bitcast.12, bf16[64,256]{1,0:T(8,128)(2,1)} %w_project_hbm.1, ...), custom_call_target="tpu_custom_call" | custom-call | tf_op jit(solution)/shard_map/pair_kernel/pallas_call | solution.py:505
  35.7 1.9 %out_kernel.1 = (bf16[1,64,16,64]{3,2,1,0:T(8,128)(2,1)}, bf16[64,16,128]{2,1,0:T(8,128)(2,1)}) custom-call(bf16[32,16,128]{2,1,0:T(8,128)(2,1)} %get-tuple-element.4.new_ref, bf16[32,16,128]{2,1,0:T(8,128)(2,1)} %get-tuple-element.5.merged_ref, bf16[64,128]{1,0:T(8,128)(2,1)} %w_out_ref.1), custom_call_target="tpu_custom_call" | custom-call | tf_op jit(solution)/shard_map/out_kernel/pallas_call | solution.py:572

commit v6 on v5

--- a/solution.py
+++ b/solution.py
@@ -440,23 +440,17 @@
 
     pl.semaphore_wait(second_sem, 3)
 
-    def send_merged(step, carry):
-        to_templ, to_chunk = templ ^ (3 - step // 8), (chunk + 4 + step) % 8
-
-        @pl.when((to_templ != templ) | (to_chunk != chunk))
-        def _():
+    for other in (3, 2, 1, 0):
+        for away in (4, 5, 3, 6, 2, 7, 1, 0) if other else (4, 5, 3, 6, 2, 7, 1):
+            to_chunk = (chunk + away) % 8
             pltpu.make_async_remote_copy(
                 src_ref=merged.at[pl.ds(pl.multiple_of(16 * to_chunk, 16), 16), :],
                 dst_ref=merged_out.at[4 * chunk + templ],
                 send_sem=merged_send,
                 recv_sem=merged_recv,
-                device_id=(to_templ, row, 8 * half + to_chunk),
+                device_id=(templ ^ other, row, 8 * half + to_chunk),
                 device_id_type=MESH,
             ).start()
-
-        return carry
-
-    lax.fori_loop(0, 32, send_merged, 0)
 
     for step in range(3):
         drain(fresh.at[0], peer_send.at[step])

time: 37.7 us -> 37.9 us (level)
  no operation moved by 1% of the time
where the time goes in v6:
time: 37.9 us; the launch traced here: 37.8 us
  Pallas kernels  37.1 us (98%)
  between operations  0.64 us (2%)
    pallas_call x1, Pallas kernels, on_device(): pl.pallas_call(pair_kernel, out_shape=(piece, piece), in_specs=[pl.BlockS...  35.2 us
    pallas_call x1, Pallas kernels, on_device(): pl.pallas_call(out_kernel, out_shape=(jax.ShapeDtypeStruct((1, 64, 16, 64...  1.94 us

profile of v6, /device:TPU:1, one launch (start us, length us, event | category | flops | bytes accessed | tf_op | source)
XLA Modules:
  0.0 37.8 jit_solution(130914993506440568)
XLA Ops:
  0.6 35.2 %pair_kernel.1 = (bf16[32,16,128]{2,1,0:T(8,128)(2,1)}, bf16[32,16,128]{2,1,0:T(8,128)(2,1)}) custom-call(bf16[64,16,64]{2,1,0:T(8,128)(2,1)} %bitcast.7, bf16[2,32,16,128]{3,2,1,0:T(8,128)(2,1)} %bitcast.8, s32[2,4]{1,0:T(2,128)} %bitcast.10, s32[2,2]{1,0:T(2,128)} %mask_hbm.1, f32[1,64]{1,0:T(1,128)} %bitcast.12, bf16[64,256]{1,0:T(8,128)(2,1)} %w_project_hbm.1, ...), custom_call_target="tpu_custom_call" | custom-call | tf_op jit(solution)/shard_map/pair_kernel/pallas_call | solution.py:499
  35.8 1.9 %out_kernel.1 = (bf16[1,64,16,64]{3,2,1,0:T(8,128)(2,1)}, bf16[64,16,128]{2,1,0:T(8,128)(2,1)}) custom-call(bf16[32,16,128]{2,1,0:T(8,128)(2,1)} %get-tuple-element.4.new_ref, bf16[32,16,128]{2,1,0:T(8,128)(2,1)} %get-tuple-element.5.merged_ref, bf16[64,128]{1,0:T(8,128)(2,1)} %w_out_ref.1), custom_call_target="tpu_custom_call" | custom-call | tf_op jit(solution)/shard_map/out_kernel/pallas_call | solution.py:566
